TPU v7x, 128 devices: a whole 4x4x4 slice. The times are simulated.
128 devices in a mesh: mp: 8 (over z_lo, x), feat: 16 (over y, z_hi, core).
Axes of the slice: x: 4, y: 4, z: 4 (z_hi: 2, z_lo: 2; z = z_hi * 2 + z_lo), core: 2. Of those that a mesh axis runs over, the one named last changes fastest.
Arguments:
- residual_in: bfloat16 [256, 3584], P(None, 'feat'), may hold values from -24 to 24
- norm_gain: float32 [3584], P('feat'), may hold values from 0.5 to 1.5
- gate_weight: bfloat16 [3584, 14336], P('feat', 'mp'), may hold values from -0.09375 to 0.09375
- up_weight: bfloat16 [3584, 14336], P('feat', 'mp'), may hold values from -0.09375 to 0.09375
- down_weight: bfloat16 [14336, 3584], P('mp', 'feat'), may hold values from -0.046875 to 0.046875
- encoder_weight: bfloat16 [3584, 65536], P(None, ('mp', 'feat')), may hold values from -0.375 to 0.375
- encoder_bias: float32 [65536], P(('mp', 'feat')), may hold values from -1.5 to 0.5
- decoder_weight: bfloat16 [65536, 3584], P(('mp', 'feat')), may hold values from -0.09375 to 0.09375
- decoder_bias: float32 [3584], replicated, may hold values from -3 to 3
Outputs:
- feature_codes: bfloat16 [256, 65536], P(None, ('mp', 'feat'))
- reconstruction: bfloat16 [256, 3584], P(('mp', 'feat'))
- encoder_gradient: bfloat16 [3584, 65536], P(None, ('mp', 'feat'))
- decoder_gradient: bfloat16 [65536, 3584], P(('mp', 'feat'))
- input_gradient: float32 [256, 3584], P(('mp', 'feat'))
All inputs are finite; a program needn't handle non-finite values.
Results may differ from a plain program's by a relative error of at most 0.023.
Values may be sent and summed in bfloat16 or wider, within the bound.
No kernel may reach another device: no remote copies, remote signals or barrier semaphores. Data moves between devices by JAX's collectives and lax.ppermute only.
A program may use at most 128 MiB of HBM per device.

v0:
```python
import jax
import jax.numpy as jnp
from jax import lax
from jax.sharding import PartitionSpec as P

D = 3584
sparsity_weight = 0.2
norm_eps = 1e-06


def shards(
    residual_in,
    norm_gain,
    gate_weight,
    up_weight,
    down_weight,
    encoder_weight,
    encoder_bias,
    decoder_weight,
    decoder_bias,
):
    rows_all = residual_in.shape[0]
    hidden_local = gate_weight.shape[1]
    rows_own = rows_all // lax.axis_size(("mp", "feat"))
    first_row = lax.axis_index(("mp", "feat")) * rows_own
    source = residual_in.astype(jnp.float32)
    squares = lax.psum(jnp.sum(source * source, axis=1), "feat")
    inverse_scale = lax.rsqrt(squares / D + norm_eps)
    normed = (source * inverse_scale[:, None] * norm_gain[None, :]).astype(jnp.bfloat16)
    joint_weight = jnp.concatenate([gate_weight, up_weight], axis=1)
    row_block = normed
    projected = lax.psum_scatter(
        jnp.dot(row_block, joint_weight, preferred_element_type=jnp.float32).astype(jnp.bfloat16),
        "feat",
        scatter_dimension=0,
        tiled=True,
    ).astype(jnp.float32)
    hidden = (jax.nn.silu(projected[:, :hidden_local]) * projected[:, hidden_local:]).astype(
        jnp.bfloat16
    )
    partial_mixed = jnp.dot(
        lax.all_gather(hidden, "feat", axis=0, tiled=True),
        down_weight,
        preferred_element_type=jnp.float32,
    )
    mixed_terms = lax.psum(partial_mixed.astype(jnp.bfloat16), "mp").astype(jnp.float32)
    stream_cols = (source + mixed_terms).astype(jnp.bfloat16)
    stream = lax.all_gather(stream_cols, "feat", axis=1, tiled=True)
    encoded = (
        jnp.dot(stream, encoder_weight, preferred_element_type=jnp.float32) + encoder_bias[None, :]
    )
    feature_codes = jax.nn.softplus(encoded).astype(jnp.bfloat16)
    partial_recon = jnp.dot(feature_codes, decoder_weight, preferred_element_type=jnp.float32)
    summed = lax.psum(partial_recon, ("mp", "feat"))
    recon_all = summed + decoder_bias[None, :]
    error = (recon_all - stream.astype(jnp.float32)).astype(jnp.bfloat16)
    recon_own = lax.dynamic_slice_in_dim(recon_all, first_row, rows_own, 0)
    error_own = lax.dynamic_slice_in_dim(error, first_row, rows_own, 0)
    decoder_gradient = lax.dot_general(
        feature_codes, error, (((0,), (0,)), ((), ())), preferred_element_type=jnp.float32
    ).astype(jnp.bfloat16)
    code_gradient = lax.dot_general(
        error, decoder_weight, (((1,), (1,)), ((), ())), preferred_element_type=jnp.float32
    )
    encoded_gradient = (jax.nn.sigmoid(encoded) * (code_gradient + sparsity_weight)).astype(
        jnp.bfloat16
    )
    encoder_gradient = lax.dot_general(
        stream, encoded_gradient, (((0,), (0,)), ((), ())), preferred_element_type=jnp.float32
    ).astype(jnp.bfloat16)
    row_block = encoded_gradient
    input_gradient = lax.psum_scatter(
        lax.dot_general(
            row_block, encoder_weight, (((1,), (1,)), ((), ())), preferred_element_type=jnp.float32
        ),
        ("mp", "feat"),
        scatter_dimension=0,
        tiled=True,
    ) - error_own.astype(jnp.float32)
    return (
        feature_codes,
        recon_own.astype(jnp.bfloat16),
        encoder_gradient,
        decoder_gradient,
        input_gradient,
    )


def solution(mesh):
    in_specs = (
        P(None, "feat"),
        P("feat"),
        P("feat", "mp"),
        P("feat", "mp"),
        P("mp", "feat"),
        P(None, ("mp", "feat")),
        P(("mp", "feat")),
        P(("mp", "feat"), None),
        P(),
    )
    out_specs = (
        P(None, ("mp", "feat")),
        P(("mp", "feat"), None),
        P(None, ("mp", "feat")),
        P(("mp", "feat"), None),
        P(("mp", "feat"), None),
    )
    return jax.shard_map(shards, mesh=mesh, in_specs=in_specs, out_specs=out_specs, check_vma=False)
```

profile of v0, /device:TPU:1, one launch (start us, length us, event | category | flops | bytes accessed | tf_op | source)
XLA Modules:
  0.0 596.9 jit_solution(6068600141430006881)
XLA Ops:
  7.2 0.0 copy-start
  7.2 0.0 reduce-scatter.3.cloned.1.call-start
  7.2 1.0 fusion.6
  8.2 35.1 %psum.21 = f32[256]{0:T(256)S(1)} all-reduce(f32[256]{0:T(256)S(1)} %fusion.6), channel_id=1, replica_groups=mesh['mp'=8,'feat'=16] {'feat'}, use_global_device_ids=true, to_apply=%region_1.0 | all-reduce | flops 256 | bytes 2048 | tf_op jit(solution)/shard_map/psum | solution.py:27
  43.3 0.0 copy-start.9
  43.3 3.5 convolution_convert_fusion.2
  46.8 0.0 reduce-scatter.3.cloned.1.call-update
  46.8 0.0 all-reduce.5.cloned.1.call-start
  46.9 69.5 %reduce-scatter.3.cloned.1.call-done = bf16[16,3584]{1,0:T(8,128)(2,1)} async-done(((bf16[256,3584]{1,0:T(8,128)(2,1)}), bf16[16,3584]{1,0:T(8,128)(2,1)}) %reduce-scatter.3.cloned.1.call-update) | async-done | bytes 114704 | tf_op jit(solution)/shard_map/reduce_scatter | solution.py:32
  116.4 0.9 convert_element_type.51
  117.3 26.6 %all_gather.6 = bf16[256,1792]{1,0:T(8,128)(2,1)S(1)} all-gather(bf16[16,1792]{1,0:T(8,128)(2,1)S(1)} %fusion.11), channel_id=1, replica_groups=mesh['mp'=8,'feat'=16] {'feat'}, dimensions={0}, use_global_device_ids=true | all-gather | bytes 974848 | tf_op jit(solution)/shard_map/all_gather | solution.py:42
  144.0 0.0 copy-done
  144.0 1.1 convolution_convert_fusion.3
  145.1 0.0 all-reduce.5.cloned.1.call-update
  145.1 0.0 all-gather.2.cloned.1.call-start
  145.2 63.2 %all-reduce.5.cloned.1.call-done = bf16[256,224]{0,1:T(8,128)(2,1)} async-done(((bf16[256,224]{0,1:T(8,128)(2,1)}), bf16[256,224]{0,1:T(8,128)(2,1)}) %all-reduce.5.cloned.1.call-update) | async-done | bytes 114704 | tf_op jit(solution)/shard_map/psum | solution.py:46
  208.3 0.0 copy-done.9
  208.3 1.6 fusion.9
  209.9 0.0 all-gather.2.cloned.1.call-update
  209.9 0.0 all-reduce.7.cloned.1.call-start
  210.0 55.2 %all-gather.2.cloned.1.call-done = bf16[256,3584]{0,1:T(8,128)(2,1)} async-done(((bf16[256,224]{0,1:T(8,128)(2,1)}), bf16[256,3584]{0,1:T(8,128)(2,1)}) %all-gather.2.cloned.1.call-update) | async-done | bytes 1835024 | tf_op jit(solution)/shard_map/all_gather | solution.py:48
  265.2 0.0 copy-done.11
  265.2 4.1 fusion.5
  269.3 0.0 copy-start.6
  269.3 0.7 copy-done.6
  270.0 0.0 copy-done.3
  270.0 3.5 fusion.15
  273.5 0.0 all-reduce.7.cloned.1.call-update
  273.5 0.0 all-reduce.9.cloned.1.call-start
  273.6 151.6 %all-reduce.7.cloned.1.call-done = f32[256,3584]{0,1:T(8,128)} async-done(((f32[256,3584]{0,1:T(8,128)}), f32[256,3584]{0,1:T(8,128)}) %all-reduce.7.cloned.1.call-update) | async-done | bytes 3670032 | tf_op jit(solution)/shard_map/psum | solution.py:54
  425.1 0.0 copy-done.1
  425.1 0.0 copy-done.10
  425.1 4.2 subtract_convert_fusion
  429.3 0.0 copy-done.4
  429.3 1.2 fusion.4
  430.5 0.1 copy-done.2
  430.6 0.7 copy-done.7
  431.3 0.8 copy-done.5
  432.1 3.0 fusion.16
  435.1 0.0 all-reduce.9.cloned.1.call-update
  435.1 1.5 dynamic-slice_convert_fusion
  436.6 0.9 copy.20
  437.5 4.6 convolution_convert_fusion
  442.2 0.0 copy-done.8
  442.2 3.0 convolution_convert_fusion.1
  445.1 141.6 %all-reduce.9.cloned.1.call-done = f32[256,3584]{0,1:T(8,128)} async-done(((f32[256,3584]{0,1:T(8,128)}), f32[256,3584]{0,1:T(8,128)}) %all-reduce.9.cloned.1.call-update) | async-done | bytes 3670032
  586.7 2.5 dynamic-slice_subtract_fusion
  589.2 1.2 copy.21
  (11 shorter events, 0.1 us)
Async XLA Ops:
  7.2 136.8 %copy-start = (bf16[1792,224]{0,1:T(8,128)(2,1)S(1)}, bf16[1792,224]{0,1:T(8,128)(2,1)}, u32[]{:S(2)}) copy-start(bf16[1792,224]{0,1:T(8,128)(2,1)} %param.13) | copy-start | bytes 2408452
  7.2 109.2 %reduce-scatter.3.cloned.1.call-start = ((), (), s32[]{:S(2)}) async-start(), calls=%async_computation.1 | async-start | bytes 1949696 | tf_op jit(solution)/shard_map/reduce_scatter | solution.py:32
  43.3 165.0 %copy-start.9 = (bf16[256,224]{0,1:T(8,128)(2,1)S(1)}, bf16[256,224]{0,1:T(8,128)(2,1)}, u32[]{:S(2)}) copy-start(bf16[256,224]{0,1:T(8,128)(2,1)} %param.9) | copy-start | bytes 344068
  46.8 218.4 %copy-start.11 = (f32[512]{0:T(512)S(1)}, f32[512]{0:T(512)}, u32[]{:S(2)}) copy-start(f32[512]{0:T(512)} %param.15) | copy-start | bytes 6148
  46.8 161.5 %all-reduce.5.cloned.1.call-start = ((), (), s32[]{:S(2)}) async-start(), calls=%async_computation.2 | async-start | bytes 229376 | tf_op jit(solution)/shard_map/psum | solution.py:46
  145.1 120.1 %all-gather.2.cloned.1.call-start = ((), (), s32[]{:S(2)}) async-start(), calls=%async_computation.3 | async-start | bytes 1949696 | tf_op jit(solution)/shard_map/all_gather | solution.py:48
  209.9 215.2 %all-reduce.7.cloned.1.call-start = ((), (), s32[]{:S(2)}) async-start(), calls=%async_computation.4 | async-start | bytes 7340032 | tf_op jit(solution)/shard_map/psum | solution.py:54
  265.2 4.8 copy-start.3
  269.3 0.7 copy-start.6
  273.5 151.6 %copy-start.1 = (bf16[256,3584]{0,1:T(8,128)(2,1)S(1)}, bf16[256,3584]{0,1:T(8,128)(2,1)}, u32[]{:S(2)}) copy-start(bf16[256,3584]{0,1:T(8,128)(2,1)} %all-gather.2.cloned.1.call-done) | copy-start | bytes 5505028
  273.5 151.6 %copy-start.10 = (f32[3584]{0:T(1024)S(1)}, f32[3584]{0:T(1024)}, u32[]{:S(2)}) copy-start(f32[3584]{0:T(1024)} %param.17) | copy-start | bytes 43012
  273.5 313.2 %all-reduce.9.cloned.1.call-start = ((), (), s32[]{:S(2)}) async-start(), calls=%async_computation.5 | async-start | bytes 7340032
  425.1 4.2 copy-start.4
  429.3 1.3 copy-start.2
  429.3 2.8 copy-start.5
  430.6 0.7 copy-start.7
  437.5 4.6 copy-start.8
Sparse Core Ops, SparseCore 0:
  47.0 69.3 reduce-scatter.2
  145.3 63.0 all-reduce.4
  211.3 53.8 all-gather.1
  273.6 151.4 all-reduce.6
  435.2 151.4 all-reduce.8
where the time goes:
time: 597 us
  waiting for transfers between devices  481 us (81%)
  blocking collectives  61.7 us (10%)
  matrix products  23.9 us (4%)
  between operations  13.9 us (2%)
  other arithmetic  10.2 us (2%)
    psum x1, waiting for transfers between devices, shards(): summed = lax.psum(partial_recon, ('mp', 'feat'))  152 us
    unnamed x6, waiting for transfers between devices  142 us
    reduce_scatter x1, waiting for transfers between devices, shards(): lax.psum_scatter(jnp.dot(row_block, joint_weight, preferred_element_type=...  69.5 us
    psum x1, waiting for transfers between devices, shards(): lax.psum(partial_mixed.astype(jnp.bfloat16), 'mp').astype(jnp.float32)  63.2 us
    all_gather x1, waiting for transfers between devices, shards(): stream = lax.all_gather(stream_cols, 'feat', axis=1, tiled=True)  55.2 us
    psum x1, blocking collectives, shards(): squares = lax.psum(jnp.sum(source * source, axis=1), 'feat')  35.1 us
    all_gather x1, blocking collectives, shards(): lax.all_gather(hidden, 'feat', axis=0, tiled=True)  26.6 us
  transfers between devices with their start and end apart: 5, of which 5 were waited for; matrix products, arithmetic and copies ran while one was open for 2% of the time, Pallas kernels for 0%

commit v1 on v0

--- a/solution.py
+++ b/solution.py
@@ -43,7 +43,9 @@
         down_weight,
         preferred_element_type=jnp.float32,
     )
-    mixed_terms = lax.psum(partial_mixed.astype(jnp.bfloat16), "mp").astype(jnp.float32)
+    mixed_terms = jnp.sum(lax.all_gather(partial_mixed.astype(jnp.bfloat16), "mp"), axis=0).astype(
+        jnp.float32
+    )
     stream_cols = (source + mixed_terms).astype(jnp.bfloat16)
     stream = lax.all_gather(stream_cols, "feat", axis=1, tiled=True)
     encoded = (

time: 597 us -> 551 us (0.923)
  waiting for transfers between devices: 481 us -> 410 us
  blocking collectives: 61.7 us -> 86.5 us
    psum x1 -> x0, waiting for transfers between devices: 63.2 us -> none  [shards(): lax.psum(partial_mixed.astype(jnp.bfloat16), 'mp').astype(jnp.float32)]
    all_gather x0 -> x1, blocking collectives: none -> 24.7 us  [shards(): lax.all_gather(partial_mixed.astype(jnp.bfloat16), 'mp')]
    unnamed x6 -> x5, waiting for transfers between devices: 142 us -> 143 us
  transfers between devices with their start and end apart: 5 -> 4, of which waited for: 5 -> 4; matrix products, arithmetic and copies ran while one was open for 2% -> 2% of each run, Pallas kernels for 0% -> 0%
where the time goes in v1:
time: 551 us; the launch traced here: 550 us
  waiting for transfers between devices  410 us (74%)
  blocking collectives  86.5 us (16%)
  matrix products  23.4 us (4%)
  between operations  13.9 us (3%)
  other arithmetic  9.47 us (2%)
  local copies, waits for them, and re-layouts  7.2 us (1%)
    psum x1, waiting for transfers between devices, shards(): summed = lax.psum(partial_recon, ('mp', 'feat'))  148 us
    unnamed x5, waiting for transfers between devices  143 us
    reduce_scatter x1, waiting for transfers between devices, shards(): lax.psum_scatter(jnp.dot(row_block, joint_weight, preferred_element_type=...  69.4 us
    all_gather x1, waiting for transfers between devices, shards(): stream = lax.all_gather(stream_cols, 'feat', axis=1, tiled=True)  49.9 us
    psum x1, blocking collectives, shards(): squares = lax.psum(jnp.sum(source * source, axis=1), 'feat')  35.1 us
    all_gather x1, blocking collectives, shards(): lax.all_gather(hidden, 'feat', axis=0, tiled=True)  26.7 us
    all_gather x1, blocking collectives, shards(): lax.all_gather(partial_mixed.astype(jnp.bfloat16), 'mp')  24.7 us
  transfers between devices with their start and end apart: 4, of which 4 were waited for; matrix products, arithmetic and copies ran while one was open for 2% of the time, Pallas kernels for 0%

profile of v1, /device:TPU:1, one launch (start us, length us, event | category | flops | bytes accessed | tf_op | source)
XLA Modules:
  0.0 550.2 jit_solution(7885201123919470868)
XLA Ops:
  7.2 0.0 copy-start
  7.2 0.0 reduce-scatter.2.cloned.1.call-start
  7.2 1.0 fusion.6
  8.2 35.1 %psum.14 = f32[256]{0:T(256)S(1)} all-reduce(f32[256]{0:T(256)S(1)} %fusion.6), channel_id=1, replica_groups=mesh['mp'=8,'feat'=16] {'feat'}, use_global_device_ids=true, to_apply=%region_1.0 | all-reduce | flops 256 | bytes 2048 | tf_op jit(solution)/shard_map/psum | solution.py:27
  43.3 3.4 convolution_convert_fusion.2
  46.8 0.0 reduce-scatter.2.cloned.1.call-update
  46.8 0.0 copy-start.7
  46.8 0.0 all-gather.3.cloned.1.call-start
  46.9 69.4 %reduce-scatter.2.cloned.1.call-done = bf16[16,3584]{1,0:T(8,128)(2,1)} async-done(((bf16[256,3584]{1,0:T(8,128)(2,1)}), bf16[16,3584]{1,0:T(8,128)(2,1)}) %reduce-scatter.2.cloned.1.call-update) | async-done | bytes 114704 | tf_op jit(solution)/shard_map/reduce_scatter | solution.py:32
  116.3 0.9 convert_element_type.53
  117.2 0.0 copy-start.9
  117.3 26.7 %all_gather.12 = bf16[256,1792]{1,0:T(8,128)(2,1)S(1)} all-gather(bf16[16,1792]{1,0:T(8,128)(2,1)S(1)} %fusion.11), channel_id=1, replica_groups=mesh['mp'=8,'feat'=16] {'feat'}, dimensions={0}, use_global_device_ids=true | all-gather | bytes 974848 | tf_op jit(solution)/shard_map/all_gather | solution.py:42
  143.9 0.0 copy-done
  143.9 0.5 convolution_convert_fusion.3
  144.4 24.7 %all-gather = bf16[2048,224]{0,1:T(8,128)(2,1)S(1)} all-gather(bf16[256,224]{0,1:T(8,128)(2,1)S(1)} %convolution_convert_fusion.3), channel_id=2, replica_groups=mesh['mp'=8,'feat'=16] {'mp'}, dimensions={0}, use_global_device_ids=true | all-gather | bytes 1032192 | tf_op jit(solution)/shard_map/all_gather | solution.py:46
  169.1 0.2 copy.16
  169.4 0.7 bitcast_reduce_fusion
  170.0 0.0 copy-done.7
  170.1 0.7 fusion.9
  170.7 0.0 all-gather.3.cloned.1.call-update
  170.8 0.0 all-reduce.4.cloned.1.call-start
  170.8 49.9 %all-gather.3.cloned.1.call-done = bf16[256,3584]{0,1:T(8,128)(2,1)} async-done(((bf16[256,224]{0,1:T(8,128)(2,1)}), bf16[256,3584]{0,1:T(8,128)(2,1)}) %all-gather.3.cloned.1.call-update) | async-done | bytes 1835024 | tf_op jit(solution)/shard_map/all_gather | solution.py:50
  220.7 0.0 copy-done.9
  220.7 0.0 copy-start.2
  220.7 4.9 fusion.5
  225.6 0.0 copy-done.2
  225.6 3.0 fusion.15
  228.5 0.0 all-reduce.4.cloned.1.call-update
  228.6 0.0 all-reduce.6.cloned.1.call-start
  228.6 1.4 copy-done.1
  230.0 2.5 copy.15
  232.6 147.5 %all-reduce.4.cloned.1.call-done = f32[256,3584]{1,0:T(8,128)} async-done(((f32[256,3584]{1,0:T(8,128)}), f32[256,3584]{1,0:T(8,128)}) %all-reduce.4.cloned.1.call-update) | async-done | bytes 3670032 | tf_op jit(solution)/shard_map/psum | solution.py:56
  380.1 0.0 copy-done.8
  380.1 4.6 subtract_convert_fusion
  384.7 0.0 copy-done.3
  384.7 0.0 copy-done.10
  384.7 0.0 copy-start.5
  384.8 1.2 fusion.4
  385.9 0.1 copy-done.4
  386.0 1.5 copy-done.5
  387.4 3.0 fusion.16
  390.5 0.0 all-reduce.6.cloned.1.call-update
  390.5 0.0 copy-done.6
  390.5 4.5 convolution_convert_fusion
  395.0 3.0 convolution_convert_fusion.1
  398.0 1.4 dynamic-slice_convert_fusion
  399.4 142.7 %all-reduce.6.cloned.1.call-done = f32[256,3584]{1,0:T(8,128)} async-done(((f32[256,3584]{1,0:T(8,128)}), f32[256,3584]{1,0:T(8,128)}) %all-reduce.6.cloned.1.call-update) | async-done | bytes 3670032
  542.1 1.5 dynamic-slice_subtract_fusion
  (8 shorter events, 0.1 us)
Async XLA Ops:
  7.2 136.8 %copy-start = (bf16[1792,224]{0,1:T(8,128)(2,1)S(1)}, bf16[1792,224]{0,1:T(8,128)(2,1)}, u32[]{:S(2)}) copy-start(bf16[1792,224]{0,1:T(8,128)(2,1)} %param.13) | copy-start | bytes 2408452
  7.2 109.1 %reduce-scatter.2.cloned.1.call-start = ((), (), s32[]{:S(2)}) async-start(), calls=%async_computation.1 | async-start | bytes 1949696 | tf_op jit(solution)/shard_map/reduce_scatter | solution.py:32
  46.8 123.2 %copy-start.7 = (bf16[256,224]{0,1:T(8,128)(2,1)S(1)}, bf16[256,224]{0,1:T(8,128)(2,1)}, u32[]{:S(2)}) copy-start(bf16[256,224]{0,1:T(8,128)(2,1)} %param.9) | copy-start | bytes 344068
  46.8 173.8 %all-gather.3.cloned.1.call-start = ((), (), s32[]{:S(2)}) async-start(), calls=%async_computation.2 | async-start | bytes 1949696 | tf_op jit(solution)/shard_map/all_gather | solution.py:50
  117.2 103.5 %copy-start.9 = (f32[512]{0:T(512)S(1)}, f32[512]{0:T(512)}, u32[]{:S(2)}) copy-start(f32[512]{0:T(512)} %param.15) | copy-start | bytes 6148
  170.8 209.4 %all-reduce.4.cloned.1.call-start = ((), (), s32[]{:S(2)}) async-start(), calls=%async_computation.3 | async-start | bytes 7340032 | tf_op jit(solution)/shard_map/psum | solution.py:56
  220.7 4.9 copy-start.2
  225.5 165.0 %copy-start.6 = (bf16[256,512]{1,0:T(8,128)(2,1)}, bf16[256,512]{1,0:T(8,128)(2,1)S(1)}, u32[]{:S(2)}) copy-start(bf16[256,512]{1,0:T(8,128)(2,1)S(1)} %get-tuple-element.7) | copy-start | bytes 786436
  228.5 1.5 copy-start.1
  228.5 151.6 %copy-start.8 = (f32[3584]{0:T(1024)S(1)}, f32[3584]{0:T(1024)}, u32[]{:S(2)}) copy-start(f32[3584]{0:T(1024)} %param.17) | copy-start | bytes 43012
  228.6 313.5 %all-reduce.6.cloned.1.call-start = ((), (), s32[]{:S(2)}) async-start(), calls=%async_computation.4 | async-start | bytes 7340032
  380.1 4.6 copy-start.3
  380.1 4.6 copy-start.10
  384.7 1.2 copy-start.4
  384.7 2.7 copy-start.5
Sparse Core Ops, SparseCore 0:
  46.9 69.3 reduce-scatter.1
  170.9 49.7 all-gather.2
  228.7 151.4 all-reduce.3
  390.6 151.4 all-reduce.5
